TPU v7x, 512 devices: a whole 4x8x8 slice. The times are simulated.
512 devices in a mesh: shard: 128 (over z_hi, x, y), tp: 4 (over z_lo, core).
Axes of the slice: x: 4, y: 8, z: 8 (z_hi: 4, z_lo: 2; z = z_hi * 2 + z_lo), core: 2. Of those that a mesh axis runs over, the one named last changes fastest.
Arguments:
- features: bfloat16 [32768, 2048], P('shard', 'tp'), may hold values from -50 to 50, as said below
- item_id: int32 [32768], P('shard'), may hold values from 0 to 262143, as said below
- w_in: bfloat16 [2048, 4096], P('shard', 'tp'), may hold values from -0.125 to 0.125
- bias_in: float32 [4096], P('tp'), may hold values from -3 to 3
- w_out: bfloat16 [1024, 4096], P('shard', 'tp'), may hold values from -16 to 16
- bias_out: float32 [1024], replicated, may hold values from -4 to 4
- item_table: bfloat16 [262144, 1024], P('shard', 'tp'), may hold values from -4 to 4
Outputs:
- new_table: bfloat16 [262144, 1024], P('shard', 'tp')
Inputs may be any that keep to these rules, and one draw needn't show every extreme that they name: `features`: feature rows of order one to sixteen. All ids differ. With owner = item_id // 2048, the 256 items of one index of shard (an aligned block) name one owner at most 4 times, and some owner is named exactly 4 times by every block.
All inputs are finite; a program needn't handle non-finite values.
Results may differ from a plain program's by a relative error of at most 0.0029.
Values may be sent and summed in bfloat16 or wider, within the bound.
No kernel may reach another device: no remote copies, remote signals or barrier semaphores. Data moves between devices by JAX's collectives and lax.ppermute only.
A program may use at most 64 MiB of HBM per device.

v0:
```python
import jax
import jax.numpy as jnp
from jax import lax
from jax.sharding import PartitionSpec as P


def tower(columns, w_in, bias_in, w_out, bias_out):
    gathered = lax.all_gather(columns, "tp", axis=1, tiled=True)
    activation = (
        jnp.dot(
            gathered,
            lax.all_gather(w_in, "shard", axis=0, tiled=True),
            preferred_element_type=jnp.float32,
        )
        + bias_in
    )
    hidden = jax.nn.silu(activation).astype(jnp.bfloat16)
    partial_out = lax.dot_general(
        hidden,
        lax.all_gather(w_out, "shard", axis=0, tiled=True),
        (((1,), (1,)), ((), ())),
        preferred_element_type=jnp.float32,
    )
    width = bias_out.shape[0]
    share_width = width // lax.axis_size("tp")
    offset = lax.axis_index("tp") * share_width
    summed = lax.psum(partial_out, "tp") + bias_out
    scaled = summed * lax.rsqrt(jnp.mean(summed * summed, axis=1, keepdims=True) + 1e-06)
    return lax.dynamic_slice_in_dim(scaled, offset, share_width, 1).astype(jnp.bfloat16)


def local(features, item_id, w_in, bias_in, w_out, bias_out, item_table):
    owners_count = lax.axis_size("shard")
    src_rows = features.shape[0]
    table_rows = item_table.shape[0]
    capacity = 2 * src_rows // owners_count
    owner_index = item_id // table_rows
    local_row = item_id - owner_index * table_rows
    owner_ids = jnp.arange(owners_count, dtype=jnp.int32)
    matches = (owner_index[:, None] == owner_ids[None, :]).astype(jnp.int32)
    within = jnp.sum((jnp.cumsum(matches, axis=0) - 1) * matches, axis=1)
    slot_index = owner_index * capacity + within
    slot_item = jnp.full((owners_count * capacity,), src_rows, jnp.int32)
    slot_item = slot_item.at[slot_index].set(jnp.arange(src_rows, dtype=jnp.int32))
    slot_rows = jnp.take(local_row, slot_item, mode="fill", fill_value=table_rows)
    slot_rows = slot_rows.reshape(owners_count, capacity)
    packed = jnp.take(features, slot_item, axis=0, mode="fill", fill_value=0)
    packed = packed.reshape(owners_count, capacity, features.shape[1])
    arrived, target_rows = (
        lax.all_to_all(packed, "shard", split_axis=0, concat_axis=0, tiled=True),
        lax.all_to_all(slot_rows, "shard", split_axis=0, concat_axis=0, tiled=True),
    )
    arrived_rows = arrived.reshape(owners_count * capacity, features.shape[1])
    embedded = tower(arrived_rows, w_in, bias_in, w_out, bias_out)
    return item_table.at[target_rows.reshape(-1)].set(embedded, mode="drop")


def solution(mesh):
    in_specs = (
        P("shard", "tp"),
        P("shard"),
        P("shard", "tp"),
        P("tp"),
        P("shard", "tp"),
        P(),
        P("shard", "tp"),
    )
    out_specs = P("shard", "tp")
    return jax.shard_map(local, mesh=mesh, in_specs=in_specs, out_specs=out_specs, check_vma=False)
```

profile of v0, /device:TPU:1, one launch (start us, length us, event | category | flops | bytes accessed | tf_op | source)
XLA Modules:
  0.0 400.6 jit_solution(10785810898543927421)
XLA Ops:
  6.5 0.0 copy-start
  6.5 0.0 copy-start.2
  6.5 0.0 all-gather.8.cloned.1.call-start
  6.5 2.3 copy.16
  8.9 0.0 all-gather.8.cloned.1.call-update
  8.9 0.0 all-gather.4.cloned.1.call-start
  8.9 0.0 copy-done.2
  9.0 0.1 copy.10
  9.1 0.2 fusion.5
  9.3 0.1 add_add_fusion
  9.4 0.2 fusion.6
  9.6 1.4 scatter_custom_fusion
  11.0 3.5 gather_fusion
  14.6 0.1 broadcast_in_dim.39
  14.7 0.0 copy-done
  14.7 2.0 gather_fusion.1
  16.7 0.1 gather.12
  16.8 0.0 copy-start.3
  16.8 0.3 broadcast_select_fusion
  17.2 40.8 %all_to_all.11 = bf16[128,4,512]{2,1,0:T(4,128)(2,1)S(1)} all-to-all(bf16[128,4,512]{2,1,0:T(4,128)(2,1)S(1)} %broadcast_select_fusion), channel_id=1, replica_groups=mesh['shard'=128,'tp'=4] {'shard'}, dimensions={0} | all-to-all | bytes 1048576 | tf_op jit(solution)/shard_map/all_to_all | solution.py:50
  57.9 0.9 reshape.102
  58.9 0.0 all-gather.4.cloned.1.call-update
  58.9 0.0 all-gather.6.cloned.1.call-start
  58.9 0.7 all-gather.6.cloned.1.call-update
  59.6 0.0 all-reduce.2.cloned.1.call-start
  59.7 79.7 %all-gather.8.cloned.1.call-done = bf16[1024,1024]{1,0:T(8,128)(2,1)} async-done(((bf16[8,1024]{1,0:T(8,128)(2,1)}), bf16[1024,1024]{1,0:T(8,128)(2,1)}) %all-gather.8.cloned.1.call-update) | async-done | bytes 2097168 | tf_op jit(solution)/shard_map/all_gather | solution.py:20
  139.4 37.1 %all-gather.4.cloned.1.call-done = bf16[512,2048]{1,0:T(8,128)(2,1)} async-done(((bf16[512,512]{1,0:T(8,128)(2,1)}), bf16[512,2048]{1,0:T(8,128)(2,1)}) %all-gather.4.cloned.1.call-update) | async-done | bytes 2097168 | tf_op jit(solution)/shard_map/all_gather | solution.py:8
  176.4 134.7 %all-gather.6.cloned.1.call-done = bf16[2048,1024]{1,0:T(8,128)(2,1)} async-done(((bf16[16,1024]{1,0:T(8,128)(2,1)}), bf16[2048,1024]{1,0:T(8,128)(2,1)}) %all-gather.6.cloned.1.call-update) | async-done | bytes 4194320 | tf_op jit(solution)/shard_map/all_gather | solution.py:12
  311.1 0.0 copy-done.3
  311.1 8.2 %fusion = f32[512,1024]{1,0:T(8,128)} fusion(bf16[1024,1024]{1,0:T(8,128)(2,1)} %all-gather.8.cloned.1.call-done, bf16[512,2048]{1,0:T(8,128)(2,1)} %all-gather.4.cloned.1.call-done, bf16[2048,1024]{1,0:T(8,128)(2,1)} %all-gather.6.cloned.1.call-done, f32[1024]{0:T(1024)S(1)} %copy-done.3), kind=kOutput, calls=%fused_computation.7 | convolution fusion | flops 3224371200 | bytes 10489856 | tf_op jit(solution)/shard_map/dot_general | solution.py:18
  319.4 0.0 copy-start.1
  319.4 0.0 all-reduce.2.cloned.1.call-update
  319.4 0.7 select_n.52
  320.1 11.9 %all-to-all-start = ((s32[128,1,4]{2,1,0:T(1,128)}), s32[128,1,4]{2,1,0:T(1,128)S(1)}, u32[]{:S(2)}, u32[]{:S(2)}) async-start(s32[128,1,4]{2,1,0:T(1,128)} %bitcast.4), calls=%async_computation | async-start | bytes 131072 | tf_op jit(solution)/shard_map/all_to_all | solution.py:51
  332.0 12.4 %all-to-all-done = s32[128,1,4]{2,1,0:T(1,128)S(1)} async-done(((s32[128,1,4]{2,1,0:T(1,128)}), s32[128,1,4]{2,1,0:T(1,128)S(1)}, u32[]{:S(2)}, u32[]{:S(2)}) %all-to-all-start) | async-done | bytes 2080 | tf_op jit(solution)/shard_map/all_to_all | solution.py:51
  344.4 0.5 broadcast.95
  344.9 0.8 reduce.3
  345.7 0.1 reshape.101
  345.9 41.5 %all-reduce.2.cloned.1.call-done = f32[512,1024]{1,0:T(8,128)} async-done(((f32[512,1024]{1,0:T(8,128)}), f32[512,1024]{1,0:T(8,128)}) %all-reduce.2.cloned.1.call-update) | async-done | bytes 2097168 | tf_op jit(solution)/shard_map/psum | solution.py:27
  387.4 0.0 copy-done.1
  387.4 1.9 multiply_reduce_fusion
  389.3 4.8 %scatter_custom_fusion.1 = bf16[2048,256]{1,0:T(8,128)(2,1)} fusion(bf16[2048,256]{1,0:T(8,128)(2,1)} %copy.16, s32[512]{0:T(512)S(1)} %bitcast.15, f32[512,1024]{1,0:T(8,128)S(1)} %get-tuple-element.6, s32[]{:T(128)} %constant.38.clone.1, s32[]{:T(128)S(6)} %select_n.55, f32[512]{0:T(512)S(1)} %add_rsqrt_fusion), kind=kCustom, calls=%fused_computation.11 | custom fusion | flops 262144 | bytes 1575428 | tf_op jit(solution)/shard_map/scatter | solution.py:55
  (12 shorter events, 0.1 us)
Async XLA Ops:
  6.5 8.2 %copy-start = (bf16[256,512]{1,0:T(8,128)(2,1)S(1)}, bf16[256,512]{1,0:T(8,128)(2,1)}, u32[]{:S(2)}) copy-start(bf16[256,512]{1,0:T(8,128)(2,1)} %param.7) | copy-start | bytes 786436
  6.5 2.4 copy-start.2
  6.5 132.8 %all-gather.8.cloned.1.call-start = ((), (), s32[]{:S(2)}) async-start(), calls=%async_computation.4 | async-start | bytes 2113536 | tf_op jit(solution)/shard_map/all_gather | solution.py:20
  8.9 167.6 %all-gather.4.cloned.1.call-start = ((), (), s32[]{:S(2)}) async-start(), calls=%async_computation.2 | async-start | bytes 2621440 | tf_op jit(solution)/shard_map/all_gather | solution.py:8
  16.8 294.3 %copy-start.3 = (f32[1024]{0:T(1024)S(1)}, f32[1024]{0:T(1024)}, u32[]{:S(2)}) copy-start(f32[1024]{0:T(1024)} %param.10) | copy-start | bytes 12292
  58.9 252.3 %all-gather.6.cloned.1.call-start = ((), (), s32[]{:S(2)}) async-start(), calls=%async_computation.3 | async-start | bytes 4227072 | tf_op jit(solution)/shard_map/all_gather | solution.py:12
  59.6 327.7 %all-reduce.2.cloned.1.call-start = ((), (), s32[]{:S(2)}) async-start(), calls=%async_computation.5 | async-start | bytes 4194304 | tf_op jit(solution)/shard_map/psum | solution.py:27
  319.4 68.0 %copy-start.1 = (f32[1024]{0:T(1024)S(1)}, f32[1024]{0:T(1024)}, u32[]{:S(2)}) copy-start(f32[1024]{0:T(1024)} %param.12) | copy-start | bytes 12292
  320.1 24.3 %all-to-all-start = ((s32[128,1,4]{2,1,0:T(1,128)}), s32[128,1,4]{2,1,0:T(1,128)S(1)}, u32[]{:S(2)}, u32[]{:S(2)}) async-start(s32[128,1,4]{2,1,0:T(1,128)} %bitcast.4), calls=%async_computation | async-start | bytes 131072 | tf_op jit(solution)/shard_map/all_to_all | solution.py:51
Sparse Core Ops, SparseCore 0:
  11.8 127.4 all-gather.7
  141.5 34.9 all-gather.3
  180.9 130.1 all-gather.5
  319.5 67.7 all-reduce.1
where the time goes:
time: 401 us
  waiting for transfers between devices  306 us (76%)
  blocking collectives  40.8 us (10%)
  between operations  13.3 us (3%)
  starting transfers between devices  12 us (3%)
  local copies, waits for them, and re-layouts  11.9 us (3%)
  other arithmetic  8.3 us (2%)
  matrix products  8.23 us (2%)
    all_gather x1, waiting for transfers between devices, tower(): lax.all_gather(w_in, 'shard', axis=0, tiled=True)  135 us
    all_gather x1, waiting for transfers between devices, tower(): lax.all_gather(w_out, 'shard', axis=0, tiled=True)  79.7 us
    psum x1, waiting for transfers between devices, tower(): summed = lax.psum(partial_out, 'tp') + bias_out  41.5 us
    all_to_all x1, blocking collectives, local(): lax.all_to_all(packed, 'shard', split_axis=0, concat_axis=0, tiled=True)  40.8 us
    all_gather x1, waiting for transfers between devices, tower(): gathered = lax.all_gather(columns, 'tp', axis=1, tiled=True)  37.1 us
    all_to_all x1, waiting for transfers between devices, local(): lax.all_to_all(slot_rows, 'shard', split_axis=0, concat_axis=0, tiled=True)  12.4 us
    all_to_all x1, starting transfers between devices, local(): lax.all_to_all(slot_rows, 'shard', split_axis=0, concat_axis=0, tiled=True)  11.9 us
    dot_general x1, matrix products, tower(): lax.dot_general(hidden, lax.all_gather(w_out, 'shard', axis=0, tiled=True...  8.23 us
  transfers between devices with their start and end apart: 5, of which 5 were waited for; matrix products, arithmetic and copies ran while one was open for 3% of the time, Pallas kernels for 0%

commit v1 on v0

--- a/solution.py
+++ b/solution.py
@@ -24,7 +24,7 @@
     width = bias_out.shape[0]
     share_width = width // lax.axis_size("tp")
     offset = lax.axis_index("tp") * share_width
-    summed = lax.psum(partial_out, "tp") + bias_out
+    summed = jnp.sum(lax.all_gather(partial_out, "tp"), axis=0) + bias_out
     scaled = summed * lax.rsqrt(jnp.mean(summed * summed, axis=1, keepdims=True) + 1e-06)
     return lax.dynamic_slice_in_dim(scaled, offset, share_width, 1).astype(jnp.bfloat16)
 

time: 401 us -> 425 us (1.060)
  waiting for transfers between devices: 306 us -> 325 us
  other arithmetic: 8.3 us -> 13.2 us
    all_gather x0 -> x1, waiting for transfers between devices: none -> 60.4 us  [tower(): summed = jnp.sum(lax.all_gather(partial_out, 'tp'), axis=0) + bias_out]
    psum x1 -> x0, waiting for transfers between devices: 41.5 us -> none  [tower(): summed = lax.psum(partial_out, 'tp') + bias_out]
    reduce_sum x0 -> x1, other arithmetic: none -> 4.65 us  [tower(): summed = jnp.sum(lax.all_gather(partial_out, 'tp'), axis=0) + bias_out]
where the time goes in v1:
time: 425 us; the launch traced here: 424 us
  waiting for transfers between devices  325 us (76%)
  blocking collectives  40.8 us (10%)
  between operations  13.3 us (3%)
  other arithmetic  13.2 us (3%)
  local copies, waits for them, and re-layouts  12 us (3%)
  starting transfers between devices  12 us (3%)
  matrix products  8.29 us (2%)
    all_gather x1, waiting for transfers between devices, tower(): lax.all_gather(w_in, 'shard', axis=0, tiled=True)  135 us
    all_gather x1, waiting for transfers between devices, tower(): lax.all_gather(w_out, 'shard', axis=0, tiled=True)  79.7 us
    all_gather x1, waiting for transfers between devices, tower(): summed = jnp.sum(lax.all_gather(partial_out, 'tp'), axis=0) + bias_out  60.4 us
    all_to_all x1, blocking collectives, local(): lax.all_to_all(packed, 'shard', split_axis=0, concat_axis=0, tiled=True)  40.8 us
    all_gather x1, waiting for transfers between devices, tower(): gathered = lax.all_gather(columns, 'tp', axis=1, tiled=True)  37.1 us
    all_to_all x1, waiting for transfers between devices, local(): lax.all_to_all(slot_rows, 'shard', split_axis=0, concat_axis=0, tiled=True)  12.4 us
    all_to_all x1, starting transfers between devices, local(): lax.all_to_all(slot_rows, 'shard', split_axis=0, concat_axis=0, tiled=True)  11.9 us
  transfers between devices with their start and end apart: 5, of which 5 were waited for; matrix products, arithmetic and copies ran while one was open for 3% of the time, Pallas kernels for 0%

profile of v1, /device:TPU:1, one launch (start us, length us, event | category | flops | bytes accessed | tf_op | source)
XLA Modules:
  0.0 424.4 jit_solution(15021890092186982375)
XLA Ops:
  6.5 0.0 copy-start
  6.5 0.0 copy-start.2
  6.5 0.0 all-gather.10.cloned.1.call-start
  6.5 2.3 copy.15
  8.9 0.0 all-gather.10.cloned.1.call-update
  8.9 0.0 all-gather.6.cloned.1.call-start
  8.9 0.0 copy-done.2
  9.0 0.1 copy.10
  9.1 0.2 fusion.5
  9.3 0.1 add_add_fusion
  9.4 0.2 fusion.6
  9.6 1.4 scatter_custom_fusion
  11.0 3.5 gather_fusion
  14.6 0.1 broadcast_in_dim.39
  14.7 0.0 copy-done
  14.7 2.0 gather_fusion.1
  16.7 0.1 gather.12
  16.8 0.0 copy-start.3
  16.8 0.3 broadcast_select_fusion
  17.2 40.8 %all_to_all.11 = bf16[128,4,512]{2,1,0:T(4,128)(2,1)S(1)} all-to-all(bf16[128,4,512]{2,1,0:T(4,128)(2,1)S(1)} %broadcast_select_fusion), channel_id=1, replica_groups=mesh['shard'=128,'tp'=4] {'shard'}, dimensions={0} | all-to-all | bytes 1048576 | tf_op jit(solution)/shard_map/all_to_all | solution.py:50
  57.9 1.0 reshape.102
  58.9 0.0 all-gather.6.cloned.1.call-update
  58.9 0.0 all-gather.8.cloned.1.call-start
  59.0 0.7 all-gather.8.cloned.1.call-update
  59.7 0.0 all-gather.12.cloned.1.call-start
  59.7 79.7 %all-gather.10.cloned.1.call-done = bf16[1024,1024]{1,0:T(8,128)(2,1)} async-done(((bf16[8,1024]{1,0:T(8,128)(2,1)}), bf16[1024,1024]{1,0:T(8,128)(2,1)}) %all-gather.10.cloned.1.call-update) | async-done | bytes 2097168 | tf_op jit(solution)/shard_map/all_gather | solution.py:20
  139.4 37.1 %all-gather.6.cloned.1.call-done = bf16[512,2048]{1,0:T(8,128)(2,1)} async-done(((bf16[512,512]{1,0:T(8,128)(2,1)}), bf16[512,2048]{1,0:T(8,128)(2,1)}) %all-gather.6.cloned.1.call-update) | async-done | bytes 2097168 | tf_op jit(solution)/shard_map/all_gather | solution.py:8
  176.4 134.7 %all-gather.8.cloned.1.call-done = bf16[2048,1024]{1,0:T(8,128)(2,1)} async-done(((bf16[16,1024]{1,0:T(8,128)(2,1)}), bf16[2048,1024]{1,0:T(8,128)(2,1)}) %all-gather.8.cloned.1.call-update) | async-done | bytes 4194320 | tf_op jit(solution)/shard_map/all_gather | solution.py:12
  311.1 0.0 copy-done.3
  311.1 8.3 %fusion = f32[512,1024]{1,0:T(8,128)} fusion(bf16[1024,1024]{1,0:T(8,128)(2,1)} %all-gather.10.cloned.1.call-done, bf16[512,2048]{1,0:T(8,128)(2,1)} %all-gather.6.cloned.1.call-done, bf16[2048,1024]{1,0:T(8,128)(2,1)} %all-gather.8.cloned.1.call-done, f32[1024]{0:T(1024)S(1)} %copy-done.3), kind=kOutput, calls=%fused_computation.7 | convolution fusion | flops 3224371200 | bytes 10489856 | tf_op jit(solution)/shard_map/dot_general | solution.py:18
  319.4 0.0 all-gather.12.cloned.1.call-update
  319.5 0.7 select_n.52
  320.2 11.9 %all-to-all-start = ((s32[128,1,4]{2,1,0:T(1,128)}), s32[128,1,4]{2,1,0:T(1,128)S(1)}, u32[]{:S(2)}, u32[]{:S(2)}) async-start(s32[128,1,4]{2,1,0:T(1,128)} %bitcast.4), calls=%async_computation | async-start | bytes 131072 | tf_op jit(solution)/shard_map/all_to_all | solution.py:51
  332.1 12.4 %all-to-all-done = s32[128,1,4]{2,1,0:T(1,128)S(1)} async-done(((s32[128,1,4]{2,1,0:T(1,128)}), s32[128,1,4]{2,1,0:T(1,128)S(1)}, u32[]{:S(2)}, u32[]{:S(2)}) %all-to-all-start) | async-done | bytes 2080 | tf_op jit(solution)/shard_map/all_to_all | solution.py:51
  344.5 0.6 broadcast.95
  345.1 0.8 reduce.3
  345.9 0.1 reshape.101
  346.0 60.4 %all-gather.12.cloned.1.call-done = f32[2048,1024]{1,0:T(8,128)} async-done(((f32[512,1024]{1,0:T(8,128)}), f32[2048,1024]{1,0:T(8,128)}) %all-gather.12.cloned.1.call-update) | async-done | bytes 8388624 | tf_op jit(solution)/shard_map/all_gather | solution.py:27
  406.4 0.0 copy-start.1
  406.4 4.7 %reduce_sum.28 = f32[512,1024]{1,0:T(8,128)S(1)} reduce(f32[4,512,1024]{2,1,0:T(8,128)} %bitcast.15, f32[]{:T(128)} %constant.72.clone.1), dimensions={0}, to_apply=%region_4.5 | reduce | flops 1572864 | bytes 10485764 | tf_op jit(solution)/shard_map/reduce_sum | solution.py:27
  411.0 0.0 copy-done.1
  411.0 1.6 multiply_reduce_fusion
  412.6 5.2 %scatter_custom_fusion.1 = bf16[2048,256]{1,0:T(8,128)(2,1)} fusion(bf16[2048,256]{1,0:T(8,128)(2,1)} %copy.15, s32[512]{0:T(512)S(1)} %bitcast.17, f32[512,1024]{1,0:T(8,128)} %get-tuple-element.6, s32[]{:T(128)} %constant.38.clone.1, s32[]{:T(128)S(6)} %select_n.55, f32[512]{0:T(512)S(1)} %add_rsqrt_fusion), kind=kCustom, calls=%fused_computation.11 | custom fusion | flops 262144 | bytes 1575428 | tf_op jit(solution)/shard_map/scatter | solution.py:55
  (12 shorter events, 0.1 us)
Async XLA Ops:
  6.5 8.2 %copy-start = (bf16[256,512]{1,0:T(8,128)(2,1)S(1)}, bf16[256,512]{1,0:T(8,128)(2,1)}, u32[]{:S(2)}) copy-start(bf16[256,512]{1,0:T(8,128)(2,1)} %param.7) | copy-start | bytes 786436
  6.5 2.4 copy-start.2
  6.5 132.8 %all-gather.10.cloned.1.call-start = ((), (), s32[]{:S(2)}) async-start(), calls=%async_computation.4 | async-start | bytes 2113536 | tf_op jit(solution)/shard_map/all_gather | solution.py:20
  8.9 167.6 %all-gather.6.cloned.1.call-start = ((), (), s32[]{:S(2)}) async-start(), calls=%async_computation.2 | async-start | bytes 2621440 | tf_op jit(solution)/shard_map/all_gather | solution.py:8
  16.8 294.3 %copy-start.3 = (f32[1024]{0:T(1024)S(1)}, f32[1024]{0:T(1024)}, u32[]{:S(2)}) copy-start(f32[1024]{0:T(1024)} %param.10) | copy-start | bytes 12292
  58.9 252.2 %all-gather.8.cloned.1.call-start = ((), (), s32[]{:S(2)}) async-start(), calls=%async_computation.3 | async-start | bytes 4227072 | tf_op jit(solution)/shard_map/all_gather | solution.py:12
  59.7 346.7 %all-gather.12.cloned.1.call-start = ((), (), s32[]{:S(2)}) async-start(), calls=%async_computation.5 | async-start | bytes 10485760 | tf_op jit(solution)/shard_map/all_gather | solution.py:27
  320.2 24.3 %all-to-all-start = ((s32[128,1,4]{2,1,0:T(1,128)}), s32[128,1,4]{2,1,0:T(1,128)S(1)}, u32[]{:S(2)}, u32[]{:S(2)}) async-start(s32[128,1,4]{2,1,0:T(1,128)} %bitcast.4), calls=%async_computation | async-start | bytes 131072 | tf_op jit(solution)/shard_map/all_to_all | solution.py:51
  406.4 4.7 %copy-start.1 = (f32[1024]{0:T(1024)S(1)}, f32[1024]{0:T(1024)}, u32[]{:S(2)}) copy-start(f32[1024]{0:T(1024)} %param.12) | copy-start | bytes 12292
Sparse Core Ops, SparseCore 0:
  11.8 127.4 all-gather.9
  141.5 34.9 all-gather.5
  180.9 130.1 all-gather.7
  319.6 86.7 all-gather.11
